TPU v7x, 32 devices: a whole 2x2x4 slice. The times are simulated.
32 devices in a mesh: slab: 4 (over y, core), angle: 8 (over z, x).
Axes of the slice: x: 2, y: 2, z: 4, core: 2. Of those that a mesh axis runs over, the one named last changes fastest.
Arguments:
- volume: float32 [1024, 128], P(('slab', 'angle')), may hold values from -6 to 6
- measured: float32 [512, 128], P('angle'), may hold values from 30 to 1000
- footprint: bfloat16 [6144, 128, 128], P(('slab', 'angle')), may hold values from 0.0099487305 to 1
- block_voxel: int32 [6144], P(('slab', 'angle')), may hold values from 0 to 255, as said below
- block_tile: int32 [6144], P(('slab', 'angle')), may hold values from 0 to 63
- block_rows: int32 [6144], P(('slab', 'angle')), may hold values from 0 to 128, as said below
Outputs:
- new_volume: float32 [1024, 128], P(('slab', 'angle'))
- weighted_residual: float32 [512, 128], P('angle')
Inputs may be any that keep to these rules, and one draw needn't show every extreme that they name: `block_rows`: 0 marks an empty slot; the live slots of each device come first, each device has at least 48 live slots, some device has all 192 live, and every device has a live slot covering all 128 rows. On each device the slots form aligned groups of 48 in a row whose voxel blocks all lie in one share block_voxel // 32, different groups of a device in different shares; so at most 48 slots of a device name one share, and in each slab one share is named by 48 slots of every device.
All inputs are finite; a program needn't handle non-finite values.
Results may differ from a plain program's by a relative error of at most 0.00042.
Values may be sent and summed in bfloat16 or wider, within the bound.
A program may use at most 64 MiB of HBM per device.

v0:
```python
import jax
import jax.numpy as jnp
from jax import lax
from jax.sharding import PartitionSpec as P


def residual_of(summed, measured_part):
    return (measured_part - summed[:, 0]) / jnp.maximum(summed[:, 1], 1.0)


def on_device(volume, measured, footprint, block_voxel, block_tile, block_rows):
    width = volume.shape[1]
    kept_blocks = volume.shape[0]
    tile_count = measured.shape[0]
    angle_count = lax.axis_size("angle")
    slab_blocks = kept_blocks * angle_count
    row_live = jnp.arange(width, dtype=jnp.int32)[None, :] < block_rows[:, None]
    coarse = volume.astype(jnp.bfloat16)
    slab_values = lax.all_gather(coarse, "angle", axis=0, tiled=True)
    picked = slab_values[block_voxel]
    stacked = jnp.stack([picked, jnp.ones_like(picked)], 1)
    forward = jnp.einsum("bpv,bkv->bkp", footprint, stacked, preferred_element_type=jnp.float32)
    forward = forward * row_live[:, None, :].astype(jnp.float32)
    tile_onehot = (block_tile[:, None] == jnp.arange(tile_count, dtype=jnp.int32)[None, :]).astype(
        jnp.float32
    )
    partial_sums = jnp.einsum("bt,bkp->tkp", tile_onehot, forward, precision=lax.Precision.HIGHEST)
    summed = lax.psum(partial_sums, "slab")
    weighted = residual_of(summed, measured)
    live_bf = row_live.astype(jnp.bfloat16)
    coarse_res = weighted.astype(jnp.bfloat16)
    res_rows = coarse_res[block_tile] * live_bf
    back_in = jnp.stack([res_rows, live_bf], 1)
    backward = jnp.einsum("bpv,bkp->bkv", footprint, back_in, preferred_element_type=jnp.float32)
    per_block = jnp.zeros((slab_blocks, 2, width), jnp.float32).at[block_voxel].add(backward)
    owned = lax.psum_scatter(per_block, "angle", scatter_dimension=0, tiled=True)
    correction = owned[:, 0] / jnp.maximum(owned[:, 1], 1.0)
    return (volume + correction, weighted)


def solution(mesh):
    in_specs = (
        P(("slab", "angle"), None),
        P("angle", None),
        P(("slab", "angle"), None, None),
        P(("slab", "angle")),
        P(("slab", "angle")),
        P(("slab", "angle")),
    )
    out_specs = (P(("slab", "angle"), None), P("angle", None))
    return jax.shard_map(
        on_device, mesh=mesh, in_specs=in_specs, out_specs=out_specs, check_vma=False
    )
```

profile of v0, /device:TPU:0, one launch (start us, length us, event | category | flops | bytes accessed | tf_op | source)
XLA Modules:
  0.0 175.8 jit_solution(4244946982530737359)
XLA Ops:
  7.2 0.0 copy-start.3
  7.2 0.0 copy-start.4
  7.2 0.0 copy-start.2
  7.2 0.0 all-reduce.5.cloned.1.call-start
  7.2 0.7 compare_select_fusion.2
  7.9 0.7 convert_element_type.25
  8.7 32.3 %all_gather.3 = bf16[256,128]{1,0:T(8,128)(2,1)S(1)} all-gather(bf16[32,128]{1,0:T(8,128)(2,1)S(1)} %convert_element_type.25), channel_id=1, replica_groups=mesh['slab'=4,'angle'=8] {'angle'}, dimensions={0}, use_global_device_ids=true | all-gather | bytes 73728 | tf_op jit(solution)/shard_map/all_gather | solution.py:19
  40.9 0.8 gather_fusion
  41.7 0.1 copy.11
  41.8 0.8 fusion.7
  42.6 0.0 copy-start.5
  42.6 0.0 copy-start.1
  42.6 6.1 %convolution_multiply_fusion = f32[192,2,128]{2,1,0:T(2,128)S(1)} fusion(bf16[192,128,128]{2,1,0:T(8,128)(2,1)} %param.8, f32[192,128]{1,0:T(8,128)S(1)} %fusion.7, bf16[192,1,128]{2,1,0:T(2,128)(2,1)S(1)} %copy.11), kind=kOutput, calls=%fused_computation.3 | convolution fusion | flops 12632064 | bytes 6635520 | tf_op jit(solution)/shard_map/bpv,bkv->bkp/dot_general | solution.py:22
  48.7 0.0 copy-done.4
  48.7 0.9 fusion
  49.6 0.0 all-reduce.5.cloned.1.call-update
  49.6 0.0 all-reduce.7.cloned.1.call-start
  49.7 0.0 copy-done.3
  49.7 0.3 compare_convert_fusion
  50.0 31.7 %all-reduce.5.cloned.1.call-done = f32[64,2,128]{2,0,1:T(8,128)} async-done(((f32[64,2,128]{2,0,1:T(8,128)}), f32[64,2,128]{2,0,1:T(8,128)}) %all-reduce.5.cloned.1.call-update) | async-done | bytes 65552 | tf_op jit(solution)/shard_map/psum | solution.py:28
  81.7 0.0 copy-done.2
  81.7 1.4 fusion.17
  83.1 0.8 gather_fusion.1
  83.9 0.3 compare_select_fusion
  84.2 4.5 %fusion.2 = f32[192,2,128]{2,1,0:T(2,128)S(1)} fusion(bf16[192,128,128]{2,1,0:T(8,128)(2,1)} %param.8, bf16[192,1,128]{2,1,0:T(2,128)(2,1)S(1)} %compare_convert_fusion, bf16[192,1,128]{2,1,0:T(2,128)(2,1)S(1)} %compare_select_fusion), kind=kOutput, calls=%fused_computation.8 | convolution fusion | flops 12779520 | bytes 6586368 | tf_op jit(solution)/shard_map/bpv,bkp->bkv/dot_general | solution.py:34
  88.7 0.1 broadcast_in_dim.6
  88.8 7.2 %scatter_fusion = f32[256,2,128]{2,1,0:T(2,128)S(1)} fusion(f32[256,2,128]{2,1,0:T(2,128)S(1)} %broadcast_in_dim.6, s32[192]{0:T(256)S(1)} %compare_select_fusion.2, f32[192,2,128]{2,1,0:T(2,128)S(1)} %fusion.2), kind=kCustom, calls=%fused_computation.2 | custom fusion | flops 49152 | bytes 590592 | tf_op jit(solution)/shard_map/scatter-add | solution.py:35
  96.0 0.0 copy-start
  96.0 0.7 copy-done
  96.7 0.0 all-reduce.7.cloned.1.call-update
  96.7 0.0 copy-done.5
  96.8 0.6 dynamic-slice
  98.0 69.5 %all-reduce.7.cloned.1.call-done = f32[256,2,128]{2,1,0:T(2,128)} async-done(((f32[256,2,128]{2,1,0:T(2,128)}), f32[256,2,128]{2,1,0:T(2,128)}) %all-reduce.7.cloned.1.call-update) | async-done | bytes 262160
  167.5 0.9 fusion.14
  168.3 0.0 copy-done.1
  168.3 0.6 add.24
  (3 shorter events, 0.0 us)
Async XLA Ops:
  7.2 42.5 %copy-start.3 = (s32[192]{0:T(256)S(1)}, s32[192]{0:T(256)}, u32[]{:S(2)}) copy-start(s32[192]{0:T(256)} %param.11) | copy-start | bytes 2308
  7.2 41.5 %copy-start.4 = (s32[192]{0:T(256)S(1)}, s32[192]{0:T(256)}, u32[]{:S(2)}) copy-start(s32[192]{0:T(256)} %param.10) | copy-start | bytes 2308
  7.2 74.5 %copy-start.2 = (f32[64,128]{1,0:T(8,128)S(1)}, f32[64,128]{1,0:T(8,128)}, u32[]{:S(2)}) copy-start(f32[64,128]{1,0:T(8,128)} %param.7) | copy-start | bytes 98308
  7.2 74.5 %all-reduce.5.cloned.1.call-start = ((), (), s32[]{:S(2)}) async-start(), calls=%async_computation | async-start | bytes 131072 | tf_op jit(solution)/shard_map/psum | solution.py:28
  42.6 54.2 %copy-start.5 = (u32[32]{0:T(128)S(1)}, u32[32]{0:T(128)}, u32[]{:S(2)}) copy-start(u32[32]{0:T(128)} %constant.19) | copy-start | bytes 388
  42.6 125.8 %copy-start.1 = (f32[32,128]{1,0:T(8,128)S(1)}, f32[32,128]{1,0:T(8,128)}, u32[]{:S(2)}) copy-start(f32[32,128]{1,0:T(8,128)} %param.6) | copy-start | bytes 49156
  49.6 117.9 %all-reduce.7.cloned.1.call-start = ((), (), s32[]{:S(2)}) async-start(), calls=%async_computation.1 | async-start | bytes 524288
  96.0 0.7 copy-start
Sparse Core Ops, SparseCore 0:
  49.7 31.9 all-reduce.4
  96.9 70.5 all-reduce.6
where the time goes:
time: 176 us
  waiting for transfers between devices  101 us (57%)
  blocking collectives  32.3 us (18%)
  between operations  14.8 us (8%)
  other arithmetic  12.8 us (7%)
  matrix products  11.5 us (7%)
  local copies, waits for them, and re-layouts  3.03 us (2%)
    unnamed x3, waiting for transfers between devices  69.5 us
    all_gather x1, blocking collectives, on_device(): slab_values = lax.all_gather(coarse, 'angle', axis=0, tiled=True)  32.3 us
    psum x1, waiting for transfers between devices, on_device(): summed = lax.psum(partial_sums, 'slab')  31.7 us
    scatter-add x1, other arithmetic, on_device(): jnp.zeros((slab_blocks, 2, width), jnp.float32).at[block_voxel]  7.22 us
    dot_general x1, matrix products, on_device(): jnp.einsum('bpv,bkv->bkp', footprint, stacked, preferred_element_type=jnp...  6.12 us
    dot_general x1, matrix products, on_device(): jnp.einsum('bpv,bkp->bkv', footprint, back_in, preferred_element_type=jnp...  4.52 us
  transfers between devices with their start and end apart: 2, of which 2 were waited for; matrix products, arithmetic and copies ran while one was open for 0% of the time, Pallas kernels for 0%

commit v1 on v0

v1 whole, which is shorter than its diff:
```python
import functools

import jax
import jax.numpy as jnp
from jax import lax
from jax.experimental import pallas as pl
from jax.experimental.pallas import tpu as pltpu
from jax.sharding import PartitionSpec as P

MESH = pl.DeviceIdType.MESH
F32 = jnp.float32
BF16 = jnp.bfloat16
FWD = 16
BWD = 12
PIECES = 4


def dot(a, b):
    return jnp.dot(a, b, preferred_element_type=F32)


def dot_nt(a, b):
    return lax.dot_general(a, b, (((1,), (1,)), ((), ())), preferred_element_type=F32)


def three_terms(x):
    hi = x.astype(BF16)
    rest = x - hi.astype(F32)
    mid = rest.astype(BF16)
    lo = (rest - mid.astype(F32)).astype(BF16)
    return hi, mid, lo


def kernel(
    n_slab, n_angle, cap,
    vol_hbm, meas_hbm, foot_hbm, voxel_hbm, tile_hbm, rows_hbm,
    new_hbm, res_hbm,
    w, vol, meas, voxel_v, tile_v, rows_v, voxel_s,
    slab_vals, picked, live, fwd, onehot_t, row_parts, proj_parts,
    col_out, col_in, back_out, back_in, res_buf, new_buf,
    piece_sem, local_sem, out_sem,
    vals_send, vals_recv, row_send, row_recv, proj_send, proj_recv,
    col_send, col_recv, back_send, back_recv,
):
    slots, width, _ = w.shape
    kept = vol.shape[0]
    tiles = meas.shape[0]
    groups = slots // cap
    piece = slots // PIECES
    my_slab = lax.axis_index("slab")
    my_angle = lax.axis_index("angle")

    def angle_peer(d):
        return lax.rem(my_angle + d, n_angle)

    def slab_peer(d):
        return lax.rem(my_slab + d, n_slab)

    vol_copy = pltpu.make_async_copy(vol_hbm, vol, local_sem.at[0])
    vol_copy.start()
    index_copies = [
        pltpu.make_async_copy(voxel_hbm, voxel_v, local_sem.at[1]),
        pltpu.make_async_copy(tile_hbm, tile_v, local_sem.at[2]),
        pltpu.make_async_copy(rows_hbm, rows_v, local_sem.at[3]),
        pltpu.make_async_copy(voxel_hbm, voxel_s, local_sem.at[4]),
    ]
    for c in index_copies:
        c.start()
    piece_copies = []
    for i in range(PIECES):
        span = pl.ds(i * piece, piece)
        c = pltpu.make_async_copy(foot_hbm.at[span], w.at[span], piece_sem.at[i])
        c.start()
        piece_copies.append(c)
    meas_copy = pltpu.make_async_copy(meas_hbm, meas, local_sem.at[5])
    meas_copy.start()

    barrier = pltpu.get_barrier_semaphore()
    for d in range(1, n_angle):
        pl.semaphore_signal(barrier, inc=1, device_id={"angle": angle_peer(d)}, device_id_type=MESH)
    for d in range(1, n_slab):
        pl.semaphore_signal(barrier, inc=1, device_id={"slab": slab_peer(d)}, device_id_type=MESH)
    vol_copy.wait()
    slab_vals[my_angle] = vol[...].astype(BF16)
    pl.semaphore_wait(barrier, n_angle + n_slab - 2)

    vals_copies = []
    for d in range(1, n_angle):
        c = pltpu.make_async_remote_copy(
            src_ref=slab_vals.at[my_angle], dst_ref=slab_vals.at[my_angle],
            send_sem=vals_send.at[d - 1], recv_sem=vals_recv.at[d - 1],
            device_id={"angle": angle_peer(d)}, device_id_type=MESH,
        )
        c.start()
        vals_copies.append(c)

    def slab_exchange(buf, send, recv):
        copies = []
        for d in range(1, n_slab):
            c = pltpu.make_async_remote_copy(
                src_ref=buf.at[my_slab], dst_ref=buf.at[my_slab],
                send_sem=send.at[d - 1], recv_sem=recv.at[d - 1],
                device_id={"slab": slab_peer(d)}, device_id_type=MESH,
            )
            c.start()
            copies.append(c)
        return copies

    def angle_exchange(out, into, send, recv):
        copies = []
        for d in range(1, n_angle):
            c = pltpu.make_async_remote_copy(
                src_ref=out.at[angle_peer(d)], dst_ref=into.at[my_angle],
                send_sem=send.at[d - 1], recv_sem=recv.at[d - 1],
                device_id={"angle": angle_peer(d)}, device_id_type=MESH,
            )
            c.start()
            copies.append(c)
        return copies

    for c in index_copies:
        c.wait()

    def down(ref):
        return jnp.broadcast_to(ref[...].astype(F32), (width, slots)).T

    voxel_col = down(voxel_v)
    tile_col = down(tile_v)
    lane = lax.broadcasted_iota(jnp.int32, (slots, width), 1).astype(F32)
    live[...] = jnp.where(lane < down(rows_v), 1.0, 0.0)
    tile_rows = lax.broadcasted_iota(jnp.int32, (tiles, slots), 0)
    onehot_t[...] = jnp.where(tile_rows == tile_v[...], 1.0, 0.0).astype(BF16)

    def scatter_tiles(values):
        terms = jnp.concatenate(three_terms(values), axis=1)
        out = dot(onehot_t[...], terms)
        return (out[:, 2 * width :] + out[:, width : 2 * width]) + out[:, :width]

    row_id = lax.broadcasted_iota(jnp.int32, (FWD, width), 0)

    def forward_step(k0, left):
        mats = w[pl.ds(k0, FWD)].reshape(FWD * width, width)
        prod = dot_nt(left, mats)
        out = prod[:, :width]
        for i in range(1, FWD):
            out = jnp.where(row_id == i, prod[:, i * width : (i + 1) * width], out)
        fwd[pl.ds(k0, FWD), :] = out

    ones = jnp.ones((FWD, width), BF16)
    for i in range(PIECES):
        piece_copies[i].wait()
        for k0 in range(i * piece, (i + 1) * piece, FWD):
            forward_step(k0, ones)
    row_parts[my_slab] = scatter_tiles(fwd[...] * live[...])
    row_copies = slab_exchange(row_parts, row_send, row_recv)

    for c in vals_copies:
        c.wait_recv()
    all_vals = slab_vals[...].reshape(n_angle * kept, width)
    sums = jnp.zeros((slots, width), F32)
    for j0 in range(0, n_angle * kept, width):
        sel = jnp.where(voxel_col == lane + float(j0), 1.0, 0.0).astype(BF16)
        sums = sums + dot(sel, all_vals[j0 : j0 + width])
    picked[...] = sums.astype(BF16)
    for k0 in range(0, slots, FWD):
        forward_step(k0, picked[pl.ds(k0, FWD), :])
    proj_parts[my_slab] = scatter_tiles(fwd[...] * live[...])
    proj_copies = slab_exchange(proj_parts, proj_send, proj_recv)

    block_id = lax.broadcasted_iota(jnp.int32, (kept, width), 0)

    def backward(rows_ref, out_ref):
        totals = []
        shares = []
        for g in range(groups):
            share = lax.div(voxel_s[0, g * cap], kept)
            ids = block_id + share * kept
            total = jnp.zeros((kept, width), F32)
            for k0 in range(g * cap, (g + 1) * cap, BWD):
                cols = []
                for k in range(k0, k0 + BWD):
                    row = jnp.broadcast_to(rows_ref[k : k + 1, :], (kept, width))
                    cols.append(jnp.where(ids == voxel_s[0, k], row, 0.0).astype(BF16))
                mats = w[pl.ds(k0, BWD)].reshape(BWD * width, width)
                total = total + dot(jnp.concatenate(cols, axis=1), mats)
            totals.append(total)
            shares.append(jnp.full((kept, width), share, jnp.int32))
        for s in range(n_angle):
            out = jnp.where(shares[0] == s, totals[0], 0.0)
            for g in range(1, groups):
                out = jnp.where(shares[g] == s, totals[g], out)
            out_ref[s] = out

    backward(live, col_out)
    col_copies = angle_exchange(col_out, col_in, col_send, col_recv)

    meas_copy.wait()
    for c in row_copies:
        c.wait()
    row_sum = row_parts[0]
    for s in range(1, n_slab):
        row_sum = row_sum + row_parts[s]
    row_sum = jnp.maximum(row_sum, 1.0)
    for c in proj_copies:
        c.wait()
    proj = proj_parts[0]
    for s in range(1, n_slab):
        proj = proj + proj_parts[s]
    weighted = (meas[...] - proj) / row_sum
    res_buf[...] = weighted
    res_copy = pltpu.make_async_copy(res_buf, res_hbm, out_sem.at[0])
    res_copy.start()
    sel = jnp.where(tile_col == lane, 1.0, 0.0)[:, :tiles].astype(BF16)
    fwd[...] = dot(sel, weighted.astype(BF16)) * live[...]
    backward(fwd, back_out)
    back_copies = angle_exchange(back_out, back_in, back_send, back_recv)

    back_in[my_angle] = back_out[my_angle]
    col_in[my_angle] = col_out[my_angle]
    for c in col_copies:
        c.wait()
    col_sum = col_in[0]
    for s in range(1, n_angle):
        col_sum = col_sum + col_in[s]
    col_sum = jnp.maximum(col_sum, 1.0)
    for c in back_copies:
        c.wait_recv()
    back = back_in[0]
    for s in range(1, n_angle):
        back = back + back_in[s]
    new_buf[...] = vol[...] + back / col_sum
    new_copy = pltpu.make_async_copy(new_buf, new_hbm, out_sem.at[1])
    new_copy.start()
    for c in vals_copies:
        c.wait_send()
    for c in back_copies:
        c.wait_send()
    res_copy.wait()
    new_copy.wait()


def on_device(volume, measured, footprint, block_voxel, block_tile, block_rows):
    n_slab = lax.axis_size("slab")
    n_angle = lax.axis_size("angle")
    kept, width = volume.shape
    tiles = measured.shape[0]
    slots = footprint.shape[0]
    cap = 2 * slots // n_angle
    dma = pltpu.SemaphoreType.DMA
    any_space = pl.BlockSpec(memory_space=pl.ANY)
    index = pltpu.VMEM((1, slots), jnp.int32)
    per_share = pltpu.VMEM((n_angle, kept, width), F32)
    per_slab = pltpu.VMEM((n_slab, tiles, width), F32)
    by_slot = pltpu.VMEM((slots, width), F32)
    return pl.pallas_call(
        functools.partial(kernel, n_slab, n_angle, cap),
        out_shape=(
            jax.ShapeDtypeStruct(volume.shape, F32),
            jax.ShapeDtypeStruct(measured.shape, F32),
        ),
        in_specs=[any_space] * 6,
        out_specs=(any_space, any_space),
        scratch_shapes=[
            pltpu.VMEM(footprint.shape, BF16),
            pltpu.VMEM(volume.shape, F32),
            pltpu.VMEM(measured.shape, F32),
            index, index, index,
            pltpu.SMEM((1, slots), jnp.int32),
            pltpu.VMEM((n_angle, kept, width), BF16),
            pltpu.VMEM((slots, width), BF16),
            by_slot, by_slot,
            pltpu.VMEM((tiles, slots), BF16),
            per_slab, per_slab,
            per_share, per_share, per_share, per_share,
            pltpu.VMEM(measured.shape, F32),
            pltpu.VMEM(volume.shape, F32),
            dma((PIECES,)), dma((6,)), dma((2,)),
            dma((n_angle - 1,)), dma((n_angle - 1,)),
            dma((n_slab - 1,)), dma((n_slab - 1,)),
            dma((n_slab - 1,)), dma((n_slab - 1,)),
            dma((n_angle - 1,)), dma((n_angle - 1,)),
            dma((n_angle - 1,)), dma((n_angle - 1,)),
        ],
        compiler_params=pltpu.CompilerParams(
            collective_id=0, has_side_effects=True, vmem_limit_bytes=56 * 1024 * 1024
        ),
        cost_estimate=pl.CostEstimate(
            flops=8 * slots * width * width, bytes_accessed=2 * slots * width * width, transcendentals=0
        ),
    )(
        volume, measured, footprint,
        block_voxel.reshape(1, slots), block_tile.reshape(1, slots), block_rows.reshape(1, slots),
    )


def solution(mesh):
    in_specs = (
        P(("slab", "angle"), None),
        P("angle", None),
        P(("slab", "angle"), None, None),
        P(("slab", "angle")),
        P(("slab", "angle")),
        P(("slab", "angle")),
    )
    out_specs = (P(("slab", "angle"), None), P("angle", None))
    return jax.shard_map(
        on_device, mesh=mesh, in_specs=in_specs, out_specs=out_specs, check_vma=False
    )
```

time: 176 us -> 26.3 us (0.15)
  waiting for transfers between devices: 101 us -> 0 us
  blocking collectives: 32.3 us -> 0 us
  Pallas kernels: 0 us -> 22.6 us
  between operations: 14.8 us -> 0.64 us
  other arithmetic: 12.8 us -> 0 us
  matrix products: 11.5 us -> 0 us
    unnamed x3 -> x0, waiting for transfers between devices: 69.5 us -> none
    all_gather x1 -> x0, blocking collectives: 32.3 us -> none  [on_device(): slab_values = lax.all_gather(coarse, 'angle', axis=0, tiled=True)]
    psum x1 -> x0, waiting for transfers between devices: 31.7 us -> none  [on_device(): summed = lax.psum(partial_sums, 'slab')]
    pallas_call x0 -> x1, Pallas kernels: none -> 22.6 us  [on_device(): pl.pallas_call(functools.partial(kernel, n_slab, n_angle, cap), out_shape...]
    dot_general x3 -> x0, matrix products: 11.5 us -> none  [the longest x1 6.12 us: on_device(): jnp.einsum('bpv,bkv->bkp', footprint, stacked, preferred_element_type=jnp...]
    scatter-add x1 -> x0, other arithmetic: 7.22 us -> none  [on_device(): jnp.zeros((slab_blocks, 2, width), jnp.float32).at[block_voxel]]
    convert_element_type x4 -> x0, other arithmetic: 3.16 us -> none  [the longest x1 1.4 us: on_device(): coarse_res = weighted.astype(jnp.bfloat16)]
  transfers between devices with their start and end apart: 2 -> 0, of which waited for: 2 -> 0; matrix products, arithmetic and copies ran while one was open for 0% -> 0% of each run, Pallas kernels for 0% -> 0%
where the time goes in v1:
time: 26.3 us; the launch traced here: 26 us
  Pallas kernels  22.6 us (86%)
  local copies, waits for them, and re-layouts  2.7 us (10%)
  between operations  0.64 us (2%)
    pallas_call x1, Pallas kernels, on_device(): pl.pallas_call(functools.partial(kernel, n_slab, n_angle, cap), out_shape...  22.6 us
    unnamed x2, local copies, waits for them, and re-layouts  2.7 us

profile of v1, /device:TPU:0, one launch (start us, length us, event | category | flops | bytes accessed | tf_op | source)
XLA Modules:
  0.0 26.0 jit_solution(5518915159879539467)
XLA Ops:
  0.6 22.6 %shard_map.77 = (f32[32,128]{1,0:T(8,128)}, f32[64,128]{1,0:T(8,128)}) custom-call(f32[32,128]{1,0:T(8,128)} %vol_hbm.1, f32[64,128]{1,0:T(8,128)} %meas_hbm.1, bf16[192,128,128]{2,1,0:T(8,128)(2,1)} %foot_hbm.1, s32[1,192]{1,0:T(1,128)} %bitcast.3, s32[1,192]{1,0:T(1,128)} %bitcast.4, s32[1,192]{1,0:T(1,128)} %bitcast.5), custom_call_target="tpu_custom_call" | custom-call | flops 25165824 | bytes 6291456 | tf_op jit(solution)/shard_map/pallas_call | solution.py:255
  23.3 1.3 %copy.10 = f32[32,128]{1,0:T(8,128)} copy(f32[32,128]{1,0:T(8,128)} %get-tuple-element.4) | data formatting | bytes 32768
  24.6 1.4 %copy.11 = f32[64,128]{1,0:T(8,128)} copy(f32[64,128]{1,0:T(8,128)} %get-tuple-element.5) | data formatting | bytes 65536

commit v2 on v1

--- a/solution.py
+++ b/solution.py
@@ -37,7 +37,7 @@
     new_hbm, res_hbm,
     w, vol, meas, voxel_v, tile_v, rows_v, voxel_s,
     slab_vals, picked, live, fwd, onehot_t, row_parts, proj_parts,
-    col_out, col_in, back_out, back_in, res_buf, new_buf,
+    col_out, col_in, back_out, back_in, res_buf, new_buf, left_live,
     piece_sem, local_sem, out_sem,
     vals_send, vals_recv, row_send, row_recv, proj_send, proj_recv,
     col_send, col_recv, back_send, back_recv,
@@ -169,7 +169,17 @@
 
     block_id = lax.broadcasted_iota(jnp.int32, (kept, width), 0)
 
-    def backward(rows_ref, out_ref):
+    def live_left(k, ids):
+        row = jnp.broadcast_to(live[k : k + 1, :], (kept, width))
+        left = jnp.where(ids == voxel_s[0, k], row, 0.0).astype(BF16)
+        left_live[k] = left
+        return left
+
+    def residual_left(k, ids):
+        row = jnp.broadcast_to(fwd[k : k + 1, :], (kept, width))
+        return left_live[k] * row.astype(BF16)
+
+    def backward(left_of, out_ref):
         totals = []
         shares = []
         for g in range(groups):
@@ -177,10 +187,7 @@
             ids = block_id + share * kept
             total = jnp.zeros((kept, width), F32)
             for k0 in range(g * cap, (g + 1) * cap, BWD):
-                cols = []
-                for k in range(k0, k0 + BWD):
-                    row = jnp.broadcast_to(rows_ref[k : k + 1, :], (kept, width))
-                    cols.append(jnp.where(ids == voxel_s[0, k], row, 0.0).astype(BF16))
+                cols = [left_of(k, ids) for k in range(k0, k0 + BWD)]
                 mats = w[pl.ds(k0, BWD)].reshape(BWD * width, width)
                 total = total + dot(jnp.concatenate(cols, axis=1), mats)
             totals.append(total)
@@ -191,7 +198,7 @@
                 out = jnp.where(shares[g] == s, totals[g], out)
             out_ref[s] = out
 
-    backward(live, col_out)
+    backward(live_left, col_out)
     col_copies = angle_exchange(col_out, col_in, col_send, col_recv)
 
     meas_copy.wait()
@@ -211,8 +218,8 @@
     res_copy = pltpu.make_async_copy(res_buf, res_hbm, out_sem.at[0])
     res_copy.start()
     sel = jnp.where(tile_col == lane, 1.0, 0.0)[:, :tiles].astype(BF16)
-    fwd[...] = dot(sel, weighted.astype(BF16)) * live[...]
-    backward(fwd, back_out)
+    fwd[...] = dot(sel, weighted.astype(BF16))
+    backward(residual_left, back_out)
     back_copies = angle_exchange(back_out, back_in, back_send, back_recv)
 
     back_in[my_angle] = back_out[my_angle]
@@ -239,6 +246,17 @@
     new_copy.wait()
 
 
+def hand_over(new_in, res_in, new_hbm, res_hbm, sem):
+    copies = [
+        pltpu.make_async_copy(new_in, new_hbm, sem.at[0]),
+        pltpu.make_async_copy(res_in, res_hbm, sem.at[1]),
+    ]
+    for c in copies:
+        c.start()
+    for c in copies:
+        c.wait()
+
+
 def on_device(volume, measured, footprint, block_voxel, block_tile, block_rows):
     n_slab = lax.axis_size("slab")
     n_angle = lax.axis_size("angle")
@@ -246,13 +264,13 @@
     tiles = measured.shape[0]
     slots = footprint.shape[0]
     cap = 2 * slots // n_angle
+    any_space = pl.BlockSpec(memory_space=pl.ANY)
     dma = pltpu.SemaphoreType.DMA
-    any_space = pl.BlockSpec(memory_space=pl.ANY)
     index = pltpu.VMEM((1, slots), jnp.int32)
     per_share = pltpu.VMEM((n_angle, kept, width), F32)
     per_slab = pltpu.VMEM((n_slab, tiles, width), F32)
     by_slot = pltpu.VMEM((slots, width), F32)
-    return pl.pallas_call(
+    new, res = pl.pallas_call(
         functools.partial(kernel, n_slab, n_angle, cap),
         out_shape=(
             jax.ShapeDtypeStruct(volume.shape, F32),
@@ -274,6 +292,7 @@
             per_share, per_share, per_share, per_share,
             pltpu.VMEM(measured.shape, F32),
             pltpu.VMEM(volume.shape, F32),
+            pltpu.VMEM((slots, kept, width), BF16),
             dma((PIECES,)), dma((6,)), dma((2,)),
             dma((n_angle - 1,)), dma((n_angle - 1,)),
             dma((n_slab - 1,)), dma((n_slab - 1,)),
@@ -291,6 +310,17 @@
         volume, measured, footprint,
         block_voxel.reshape(1, slots), block_tile.reshape(1, slots), block_rows.reshape(1, slots),
     )
+    return pl.pallas_call(
+        hand_over,
+        out_shape=(
+            jax.ShapeDtypeStruct(volume.shape, F32),
+            jax.ShapeDtypeStruct(measured.shape, F32),
+        ),
+        in_specs=[any_space] * 2,
+        out_specs=(any_space, any_space),
+        scratch_shapes=[dma((2,))],
+        compiler_params=pltpu.CompilerParams(vmem_limit_bytes=56 * 1024 * 1024),
+    )(new, res)
 
 
 def solution(mesh):

time: 26.3 us -> 26.2 us (level)
  local copies, waits for them, and re-layouts: 2.7 us -> 0 us
  Pallas kernels: 22.6 us -> 25.3 us
    unnamed x2 -> x0, local copies, waits for them, and re-layouts: 2.7 us -> none
    pallas_call x0 -> x1, Pallas kernels: none -> 2.61 us  [on_device(): pl.pallas_call(hand_over, out_shape=(jax.ShapeDtypeStruct(volume.shape, F...]
where the time goes in v2:
time: 26.2 us; the launch traced here: 25.9 us
  Pallas kernels  25.3 us (97%)
  between operations  0.64 us (2%)
    pallas_call x1, Pallas kernels, on_device(): pl.pallas_call(functools.partial(kernel, n_slab, n_angle, cap), out_shape...  22.7 us
    pallas_call x1, Pallas kernels, on_device(): pl.pallas_call(hand_over, out_shape=(jax.ShapeDtypeStruct(volume.shape, F...  2.61 us

profile of v2, /device:TPU:0, one launch (start us, length us, event | category | flops | bytes accessed | tf_op | source)
XLA Modules:
  0.0 25.9 jit_solution(11201973126997426783)
XLA Ops:
  0.6 22.7 %shard_map.77 = (f32[32,128]{1,0:T(8,128)}, f32[64,128]{1,0:T(8,128)}) custom-call(f32[32,128]{1,0:T(8,128)} %vol_hbm.1, f32[64,128]{1,0:T(8,128)} %meas_hbm.1, bf16[192,128,128]{2,1,0:T(8,128)(2,1)} %foot_hbm.1, s32[1,192]{1,0:T(1,128)} %bitcast.3, s32[1,192]{1,0:T(1,128)} %bitcast.4, s32[1,192]{1,0:T(1,128)} %bitcast.5), custom_call_target="tpu_custom_call" | custom-call | flops 25165824 | bytes 6291456 | tf_op jit(solution)/shard_map/pallas_call | solution.py:273
  23.3 2.6 %shard_map.78 = (f32[32,128]{1,0:T(8,128)}, f32[64,128]{1,0:T(8,128)}) custom-call(f32[32,128]{1,0:T(8,128)} %get-tuple-element.4.new_in, f32[64,128]{1,0:T(8,128)} %get-tuple-element.5.res_in), custom_call_target="tpu_custom_call" | custom-call | tf_op jit(solution)/shard_map/pallas_call | solution.py:313

commit v3 on v2

--- a/solution.py
+++ b/solution.py
@@ -19,10 +19,6 @@
     return jnp.dot(a, b, preferred_element_type=F32)
 
 
-def dot_nt(a, b):
-    return lax.dot_general(a, b, (((1,), (1,)), ((), ())), preferred_element_type=F32)
-
-
 def three_terms(x):
     hi = x.astype(BF16)
     rest = x - hi.astype(F32)
@@ -35,7 +31,7 @@
     n_slab, n_angle, cap,
     vol_hbm, meas_hbm, foot_hbm, voxel_hbm, tile_hbm, rows_hbm,
     new_hbm, res_hbm,
-    w, vol, meas, voxel_v, tile_v, rows_v, voxel_s,
+    w, w_turned, vol, meas, voxel_v, tile_v, rows_v, voxel_s,
     slab_vals, picked, live, fwd, onehot_t, row_parts, proj_parts,
     col_out, col_in, back_out, back_in, res_buf, new_buf, left_live,
     piece_sem, local_sem, out_sem,
@@ -137,20 +133,18 @@
         return (out[:, 2 * width :] + out[:, width : 2 * width]) + out[:, :width]
 
     row_id = lax.broadcasted_iota(jnp.int32, (FWD, width), 0)
+    own_row = [jnp.where(row_id == i, 1.0, 0.0).astype(BF16) for i in range(FWD)]
 
     def forward_step(k0, left):
-        mats = w[pl.ds(k0, FWD)].reshape(FWD * width, width)
-        prod = dot_nt(left, mats)
-        out = prod[:, :width]
-        for i in range(1, FWD):
-            out = jnp.where(row_id == i, prod[:, i * width : (i + 1) * width], out)
-        fwd[pl.ds(k0, FWD), :] = out
-
-    ones = jnp.ones((FWD, width), BF16)
+        mats = w_turned[pl.ds(k0, FWD)].reshape(FWD * width, width)
+        fwd[pl.ds(k0, FWD), :] = dot(jnp.concatenate(left, axis=1), mats)
+
     for i in range(PIECES):
         piece_copies[i].wait()
         for k0 in range(i * piece, (i + 1) * piece, FWD):
-            forward_step(k0, ones)
+            for k in range(k0, k0 + FWD):
+                w_turned[k] = w[k].T
+            forward_step(k0, own_row)
     row_parts[my_slab] = scatter_tiles(fwd[...] * live[...])
     row_copies = slab_exchange(row_parts, row_send, row_recv)
 
@@ -163,7 +157,8 @@
         sums = sums + dot(sel, all_vals[j0 : j0 + width])
     picked[...] = sums.astype(BF16)
     for k0 in range(0, slots, FWD):
-        forward_step(k0, picked[pl.ds(k0, FWD), :])
+        rows = picked[pl.ds(k0, FWD), :]
+        forward_step(k0, [rows * own for own in own_row])
     proj_parts[my_slab] = scatter_tiles(fwd[...] * live[...])
     proj_copies = slab_exchange(proj_parts, proj_send, proj_recv)
 
@@ -235,7 +230,7 @@
     back = back_in[0]
     for s in range(1, n_angle):
         back = back + back_in[s]
-    new_buf[...] = vol[...] + back / col_sum
+    new_buf[...] = back / col_sum
     new_copy = pltpu.make_async_copy(new_buf, new_hbm, out_sem.at[1])
     new_copy.start()
     for c in vals_copies:
@@ -244,17 +239,6 @@
         c.wait_send()
     res_copy.wait()
     new_copy.wait()
-
-
-def hand_over(new_in, res_in, new_hbm, res_hbm, sem):
-    copies = [
-        pltpu.make_async_copy(new_in, new_hbm, sem.at[0]),
-        pltpu.make_async_copy(res_in, res_hbm, sem.at[1]),
-    ]
-    for c in copies:
-        c.start()
-    for c in copies:
-        c.wait()
 
 
 def on_device(volume, measured, footprint, block_voxel, block_tile, block_rows):
@@ -279,6 +263,7 @@
         in_specs=[any_space] * 6,
         out_specs=(any_space, any_space),
         scratch_shapes=[
+            pltpu.VMEM(footprint.shape, BF16),
             pltpu.VMEM(footprint.shape, BF16),
             pltpu.VMEM(volume.shape, F32),
             pltpu.VMEM(measured.shape, F32),
@@ -310,17 +295,7 @@
         volume, measured, footprint,
         block_voxel.reshape(1, slots), block_tile.reshape(1, slots), block_rows.reshape(1, slots),
     )
-    return pl.pallas_call(
-        hand_over,
-        out_shape=(
-            jax.ShapeDtypeStruct(volume.shape, F32),
-            jax.ShapeDtypeStruct(measured.shape, F32),
-        ),
-        in_specs=[any_space] * 2,
-        out_specs=(any_space, any_space),
-        scratch_shapes=[dma((2,))],
-        compiler_params=pltpu.CompilerParams(vmem_limit_bytes=56 * 1024 * 1024),
-    )(new, res)
+    return volume + new, res
 
 
 def solution(mesh):

time: 26.2 us -> 25.4 us (0.969)
  Pallas kernels: 25.3 us -> 21.8 us
  local copies, waits for them, and re-layouts: 0 us -> 1.38 us
  other arithmetic: 0 us -> 1.33 us
    pallas_call x1 -> x0, Pallas kernels: 2.61 us -> none  [on_device(): pl.pallas_call(hand_over, out_shape=(jax.ShapeDtypeStruct(volume.shape, F...]
    unnamed x0 -> x3, local copies, waits for them, and re-layouts: none -> 1.38 us
    add x0 -> x1, other arithmetic: none -> 1.33 us  [on_device(): return (volume + new, res)]
    pallas_call x1, Pallas kernels: 22.7 us -> 21.8 us  [on_device(): pl.pallas_call(functools.partial(kernel, n_slab, n_angle, cap), out_shape...]
where the time goes in v3:
time: 25.4 us; the launch traced here: 25.2 us
  Pallas kernels  21.8 us (86%)
  local copies, waits for them, and re-layouts  1.38 us (5%)
  other arithmetic  1.33 us (5%)
  between operations  0.66 us (3%)
    pallas_call x1, Pallas kernels, on_device(): pl.pallas_call(functools.partial(kernel, n_slab, n_angle, cap), out_shape...  21.8 us
    unnamed x3, local copies, waits for them, and re-layouts  1.38 us
    add x1, other arithmetic, on_device(): return (volume + new, res)  1.33 us

profile of v3, /device:TPU:0, one launch (start us, length us, event | category | flops | bytes accessed | tf_op | source)
XLA Modules:
  0.0 25.2 jit_solution(10753108174439585240)
XLA Ops:
  0.6 0.0 copy-start
  0.6 21.8 %shard_map.77 = (f32[32,128]{1,0:T(8,128)}, f32[64,128]{1,0:T(8,128)}) custom-call(f32[32,128]{1,0:T(8,128)} %vol_hbm.1, f32[64,128]{1,0:T(8,128)} %meas_hbm.1, bf16[192,128,128]{2,1,0:T(8,128)(2,1)} %foot_hbm.1, s32[1,192]{1,0:T(1,128)} %bitcast.3, s32[1,192]{1,0:T(1,128)} %bitcast.4, s32[1,192]{1,0:T(1,128)} %bitcast.5), custom_call_target="tpu_custom_call" | custom-call | flops 25165824 | bytes 6291456 | tf_op jit(solution)/shard_map/pallas_call | solution.py:257
  22.5 0.0 copy-done
  22.5 1.3 %add.3 = f32[32,128]{1,0:T(8,128)} add(f32[32,128]{1,0:T(8,128)S(1)} %copy-done, f32[32,128]{1,0:T(8,128)} %get-tuple-element.4) | non-fusion elementwise | flops 4096 | bytes 49152 | tf_op jit(solution)/shard_map/add | solution.py:298
  23.8 1.4 %copy.9 = f32[64,128]{1,0:T(8,128)} copy(f32[64,128]{1,0:T(8,128)} %get-tuple-element.9) | data formatting | bytes 65536
Async XLA Ops:
  0.6 21.8 %copy-start = (f32[32,128]{1,0:T(8,128)S(1)}, f32[32,128]{1,0:T(8,128)}, u32[]{:S(2)}) copy-start(f32[32,128]{1,0:T(8,128)} %vol_hbm.1) | copy-start | bytes 49156

commit v4 on v3

--- a/solution.py
+++ b/solution.py
@@ -46,6 +46,8 @@
     my_slab = lax.axis_index("slab")
     my_angle = lax.axis_index("angle")
 
+    far_first = sorted(range(1, n_angle), key=lambda d: -min(d, n_angle - d))
+
     def angle_peer(d):
         return lax.rem(my_angle + d, n_angle)
 
@@ -81,7 +83,7 @@
     pl.semaphore_wait(barrier, n_angle + n_slab - 2)
 
     vals_copies = []
-    for d in range(1, n_angle):
+    for d in far_first:
         c = pltpu.make_async_remote_copy(
             src_ref=slab_vals.at[my_angle], dst_ref=slab_vals.at[my_angle],
             send_sem=vals_send.at[d - 1], recv_sem=vals_recv.at[d - 1],
@@ -104,7 +106,7 @@
 
     def angle_exchange(out, into, send, recv):
         copies = []
-        for d in range(1, n_angle):
+        for d in far_first:
             c = pltpu.make_async_remote_copy(
                 src_ref=out.at[angle_peer(d)], dst_ref=into.at[my_angle],
                 send_sem=send.at[d - 1], recv_sem=recv.at[d - 1],
@@ -170,11 +172,7 @@
         left_live[k] = left
         return left
 
-    def residual_left(k, ids):
-        row = jnp.broadcast_to(fwd[k : k + 1, :], (kept, width))
-        return left_live[k] * row.astype(BF16)
-
-    def backward(left_of, out_ref):
+    def live_sums(out_ref):
         totals = []
         shares = []
         for g in range(groups):
@@ -182,7 +180,7 @@
             ids = block_id + share * kept
             total = jnp.zeros((kept, width), F32)
             for k0 in range(g * cap, (g + 1) * cap, BWD):
-                cols = [left_of(k, ids) for k in range(k0, k0 + BWD)]
+                cols = [live_left(k, ids) for k in range(k0, k0 + BWD)]
                 mats = w[pl.ds(k0, BWD)].reshape(BWD * width, width)
                 total = total + dot(jnp.concatenate(cols, axis=1), mats)
             totals.append(total)
@@ -193,7 +191,7 @@
                 out = jnp.where(shares[g] == s, totals[g], out)
             out_ref[s] = out
 
-    backward(live_left, col_out)
+    live_sums(col_out)
     col_copies = angle_exchange(col_out, col_in, col_send, col_recv)
 
     meas_copy.wait()
@@ -214,10 +212,37 @@
     res_copy.start()
     sel = jnp.where(tile_col == lane, 1.0, 0.0)[:, :tiles].astype(BF16)
     fwd[...] = dot(sel, weighted.astype(BF16))
-    backward(residual_left, back_out)
-    back_copies = angle_exchange(back_out, back_in, back_send, back_recv)
-
-    back_in[my_angle] = back_out[my_angle]
+    group_shares = [lax.div(voxel_s[0, g * cap], kept) for g in range(groups)]
+
+    def residual_sums(share):
+        first = jnp.int32(0)
+        named = jnp.float32(0.0)
+        for g in range(groups):
+            here = group_shares[g] == share
+            first = jnp.where(here, g * cap, first)
+            named = jnp.where(here, 1.0, named)
+        total = jnp.zeros((kept, width), F32)
+        for k0 in range(0, cap, BWD):
+            cols = []
+            for k in range(k0, k0 + BWD):
+                row = jnp.broadcast_to(fwd[pl.ds(first + k, 1), :], (kept, width))
+                cols.append(left_live[first + k] * row.astype(BF16))
+            mats = w[pl.ds(first + k0, BWD)].reshape(BWD * width, width)
+            total = total + dot(jnp.concatenate(cols, axis=1), mats)
+        return total * named
+
+    back_copies = []
+    for d in far_first:
+        back_out[d] = residual_sums(angle_peer(d))
+        c = pltpu.make_async_remote_copy(
+            src_ref=back_out.at[d], dst_ref=back_in.at[my_angle],
+            send_sem=back_send.at[d - 1], recv_sem=back_recv.at[d - 1],
+            device_id={"angle": angle_peer(d)}, device_id_type=MESH,
+        )
+        c.start()
+        back_copies.append(c)
+    back_in[my_angle] = residual_sums(my_angle)
+
     col_in[my_angle] = col_out[my_angle]
     for c in col_copies:
         c.wait()

time: 25.4 us -> 26.5 us (1.043)
  Pallas kernels: 21.8 us -> 22.9 us
    pallas_call x1, Pallas kernels: 21.8 us -> 22.9 us  [on_device(): pl.pallas_call(functools.partial(kernel, n_slab, n_angle, cap), out_shape...]
where the time goes in v4:
time: 26.5 us; the launch traced here: 26.2 us
  Pallas kernels  22.9 us (86%)
  local copies, waits for them, and re-layouts  1.38 us (5%)
  other arithmetic  1.33 us (5%)
  between operations  0.66 us (2%)
    pallas_call x1, Pallas kernels, on_device(): pl.pallas_call(functools.partial(kernel, n_slab, n_angle, cap), out_shape...  22.9 us
    unnamed x3, local copies, waits for them, and re-layouts  1.38 us
    add x1, other arithmetic, on_device(): return (volume + new, res)  1.33 us

profile of v4, /device:TPU:0, one launch (start us, length us, event | category | flops | bytes accessed | tf_op | source)
XLA Modules:
  0.0 26.2 jit_solution(48574843150001432)
XLA Ops:
  0.6 0.0 copy-start
  0.6 22.9 %shard_map.77 = (f32[32,128]{1,0:T(8,128)}, f32[64,128]{1,0:T(8,128)}) custom-call(f32[32,128]{1,0:T(8,128)} %vol_hbm.1, f32[64,128]{1,0:T(8,128)} %meas_hbm.1, bf16[192,128,128]{2,1,0:T(8,128)(2,1)} %foot_hbm.1, s32[1,192]{1,0:T(1,128)} %bitcast.3, s32[1,192]{1,0:T(1,128)} %bitcast.4, s32[1,192]{1,0:T(1,128)} %bitcast.5), custom_call_target="tpu_custom_call" | custom-call | flops 25165824 | bytes 6291456 | tf_op jit(solution)/shard_map/pallas_call | solution.py:282
  23.5 0.0 copy-done
  23.5 1.3 %add.3 = f32[32,128]{1,0:T(8,128)} add(f32[32,128]{1,0:T(8,128)S(1)} %copy-done, f32[32,128]{1,0:T(8,128)} %get-tuple-element.4) | non-fusion elementwise | flops 4096 | bytes 49152 | tf_op jit(solution)/shard_map/add | solution.py:323
  24.9 1.4 %copy.9 = f32[64,128]{1,0:T(8,128)} copy(f32[64,128]{1,0:T(8,128)} %get-tuple-element.9) | data formatting | bytes 65536
Async XLA Ops:
  0.6 22.9 %copy-start = (f32[32,128]{1,0:T(8,128)S(1)}, f32[32,128]{1,0:T(8,128)}, u32[]{:S(2)}) copy-start(f32[32,128]{1,0:T(8,128)} %vol_hbm.1) | copy-start | bytes 49156

commit v5 on v3

--- a/solution.py
+++ b/solution.py
@@ -11,7 +11,7 @@
 F32 = jnp.float32
 BF16 = jnp.bfloat16
 FWD = 16
-BWD = 12
+BWD = 6
 PIECES = 4
 
 
@@ -46,6 +46,8 @@
     my_slab = lax.axis_index("slab")
     my_angle = lax.axis_index("angle")
 
+    far_first = sorted(range(1, n_angle), key=lambda d: -min(d, n_angle - d))
+
     def angle_peer(d):
         return lax.rem(my_angle + d, n_angle)
 
@@ -81,7 +83,7 @@
     pl.semaphore_wait(barrier, n_angle + n_slab - 2)
 
     vals_copies = []
-    for d in range(1, n_angle):
+    for d in far_first:
         c = pltpu.make_async_remote_copy(
             src_ref=slab_vals.at[my_angle], dst_ref=slab_vals.at[my_angle],
             send_sem=vals_send.at[d - 1], recv_sem=vals_recv.at[d - 1],
@@ -104,7 +106,7 @@
 
     def angle_exchange(out, into, send, recv):
         copies = []
-        for d in range(1, n_angle):
+        for d in far_first:
             c = pltpu.make_async_remote_copy(
                 src_ref=out.at[angle_peer(d)], dst_ref=into.at[my_angle],
                 send_sem=send.at[d - 1], recv_sem=recv.at[d - 1],
@@ -133,11 +135,20 @@
         return (out[:, 2 * width :] + out[:, width : 2 * width]) + out[:, :width]
 
     row_id = lax.broadcasted_iota(jnp.int32, (FWD, width), 0)
-    own_row = [jnp.where(row_id == i, 1.0, 0.0).astype(BF16) for i in range(FWD)]
+    half = FWD // 2
+    own_row = [
+        jnp.where((row_id == i) | (row_id == i + half), 1.0, 0.0).astype(BF16) for i in range(half)
+    ]
+
+    def side_by_side(ref, k0, count):
+        return jnp.concatenate(
+            [ref[pl.ds(k, count)].reshape(count * width, width) for k in (k0, k0 + count)], axis=1
+        )
 
     def forward_step(k0, left):
-        mats = w_turned[pl.ds(k0, FWD)].reshape(FWD * width, width)
-        fwd[pl.ds(k0, FWD), :] = dot(jnp.concatenate(left, axis=1), mats)
+        prod = dot(jnp.concatenate(left, axis=1), side_by_side(w_turned, k0, half))
+        fwd[pl.ds(k0, half), :] = prod[:half, :width]
+        fwd[pl.ds(k0 + half, half), :] = prod[half:, width:]
 
     for i in range(PIECES):
         piece_copies[i].wait()
@@ -181,10 +192,13 @@
             share = lax.div(voxel_s[0, g * cap], kept)
             ids = block_id + share * kept
             total = jnp.zeros((kept, width), F32)
-            for k0 in range(g * cap, (g + 1) * cap, BWD):
-                cols = [left_of(k, ids) for k in range(k0, k0 + BWD)]
-                mats = w[pl.ds(k0, BWD)].reshape(BWD * width, width)
-                total = total + dot(jnp.concatenate(cols, axis=1), mats)
+            for k0 in range(g * cap, (g + 1) * cap, 2 * BWD):
+                left = [
+                    jnp.concatenate([left_of(k + i, ids) for i in range(BWD)], axis=1)
+                    for k in (k0, k0 + BWD)
+                ]
+                prod = dot(jnp.concatenate(left, axis=0), side_by_side(w, k0, BWD))
+                total = total + (prod[:kept, :width] + prod[kept:, width:])
             totals.append(total)
             shares.append(jnp.full((kept, width), share, jnp.int32))
         for s in range(n_angle):

time: 25.4 us -> 27 us (1.063)
  Pallas kernels: 21.8 us -> 23.4 us
    pallas_call x1, Pallas kernels: 21.8 us -> 23.4 us  [on_device(): pl.pallas_call(functools.partial(kernel, n_slab, n_angle, cap), out_shape...]
where the time goes in v5:
time: 27 us; the launch traced here: 26.8 us
  Pallas kernels  23.4 us (87%)
  local copies, waits for them, and re-layouts  1.38 us (5%)
  other arithmetic  1.33 us (5%)
  between operations  0.66 us (2%)
    pallas_call x1, Pallas kernels, on_device(): pl.pallas_call(functools.partial(kernel, n_slab, n_angle, cap), out_shape...  23.4 us
    unnamed x3, local copies, waits for them, and re-layouts  1.38 us
    add x1, other arithmetic, on_device(): return (volume + new, res)  1.33 us

profile of v5, /device:TPU:0, one launch (start us, length us, event | category | flops | bytes accessed | tf_op | source)
XLA Modules:
  0.0 26.8 jit_solution(10200472527597684754)
XLA Ops:
  0.6 0.0 copy-start
  0.6 23.4 %shard_map.77 = (f32[32,128]{1,0:T(8,128)}, f32[64,128]{1,0:T(8,128)}) custom-call(f32[32,128]{1,0:T(8,128)} %vol_hbm.1, f32[64,128]{1,0:T(8,128)} %meas_hbm.1, bf16[192,128,128]{2,1,0:T(8,128)(2,1)} %foot_hbm.1, s32[1,192]{1,0:T(1,128)} %bitcast.3, s32[1,192]{1,0:T(1,128)} %bitcast.4, s32[1,192]{1,0:T(1,128)} %bitcast.5), custom_call_target="tpu_custom_call" | custom-call | flops 25165824 | bytes 6291456 | tf_op jit(solution)/shard_map/pallas_call | solution.py:271
  24.1 0.0 copy-done
  24.1 1.3 %add.3 = f32[32,128]{1,0:T(8,128)} add(f32[32,128]{1,0:T(8,128)S(1)} %copy-done, f32[32,128]{1,0:T(8,128)} %get-tuple-element.4) | non-fusion elementwise | flops 4096 | bytes 49152 | tf_op jit(solution)/shard_map/add | solution.py:312
  25.4 1.4 %copy.9 = f32[64,128]{1,0:T(8,128)} copy(f32[64,128]{1,0:T(8,128)} %get-tuple-element.9) | data formatting | bytes 65536
Async XLA Ops:
  0.6 23.4 %copy-start = (f32[32,128]{1,0:T(8,128)S(1)}, f32[32,128]{1,0:T(8,128)}, u32[]{:S(2)}) copy-start(f32[32,128]{1,0:T(8,128)} %vol_hbm.1) | copy-start | bytes 49156

commit v6 on v5

--- a/solution.py
+++ b/solution.py
@@ -46,10 +46,18 @@
     my_slab = lax.axis_index("slab")
     my_angle = lax.axis_index("angle")
 
-    far_first = sorted(range(1, n_angle), key=lambda d: -min(d, n_angle - d))
+    far_first = range(n_angle - 1, 0, -1)
 
     def angle_peer(d):
-        return lax.rem(my_angle + d, n_angle)
+        if n_angle & (n_angle - 1):
+            return lax.rem(my_angle + d, n_angle)
+        peer = my_angle
+        bit = 1
+        while bit < n_angle:
+            if d & bit:
+                peer = peer + bit * (1 - 2 * lax.rem(lax.div(my_angle, bit), 2))
+            bit *= 2
+        return peer
 
     def slab_peer(d):
         return lax.rem(my_slab + d, n_slab)

time: 27 us -> 26.4 us (0.978)
  Pallas kernels: 23.4 us -> 22.8 us
    pallas_call x1, Pallas kernels: 23.4 us -> 22.8 us  [on_device(): pl.pallas_call(functools.partial(kernel, n_slab, n_angle, cap), out_shape...]
where the time goes in v6:
time: 26.4 us; the launch traced here: 26.2 us
  Pallas kernels  22.8 us (86%)
  local copies, waits for them, and re-layouts  1.38 us (5%)
  other arithmetic  1.33 us (5%)
  between operations  0.66 us (2%)
    pallas_call x1, Pallas kernels, on_device(): pl.pallas_call(functools.partial(kernel, n_slab, n_angle, cap), out_shape...  22.8 us
    unnamed x3, local copies, waits for them, and re-layouts  1.38 us
    add x1, other arithmetic, on_device(): return (volume + new, res)  1.33 us

profile of v6, /device:TPU:0, one launch (start us, length us, event | category | flops | bytes accessed | tf_op | source)
XLA Modules:
  0.0 26.2 jit_solution(17218017937128288674)
XLA Ops:
  0.6 0.0 copy-start
  0.6 22.8 %shard_map.77 = (f32[32,128]{1,0:T(8,128)}, f32[64,128]{1,0:T(8,128)}) custom-call(f32[32,128]{1,0:T(8,128)} %vol_hbm.1, f32[64,128]{1,0:T(8,128)} %meas_hbm.1, bf16[192,128,128]{2,1,0:T(8,128)(2,1)} %foot_hbm.1, s32[1,192]{1,0:T(1,128)} %bitcast.3, s32[1,192]{1,0:T(1,128)} %bitcast.4, s32[1,192]{1,0:T(1,128)} %bitcast.5), custom_call_target="tpu_custom_call" | custom-call | flops 25165824 | bytes 6291456 | tf_op jit(solution)/shard_map/pallas_call | solution.py:279
  23.5 0.0 copy-done
  23.5 1.3 %add.3 = f32[32,128]{1,0:T(8,128)} add(f32[32,128]{1,0:T(8,128)S(1)} %copy-done, f32[32,128]{1,0:T(8,128)} %get-tuple-element.4) | non-fusion elementwise | flops 4096 | bytes 49152 | tf_op jit(solution)/shard_map/add | solution.py:320
  24.8 1.4 %copy.9 = f32[64,128]{1,0:T(8,128)} copy(f32[64,128]{1,0:T(8,128)} %get-tuple-element.9) | data formatting | bytes 65536
Async XLA Ops:
  0.6 22.9 %copy-start = (f32[32,128]{1,0:T(8,128)S(1)}, f32[32,128]{1,0:T(8,128)}, u32[]{:S(2)}) copy-start(f32[32,128]{1,0:T(8,128)} %vol_hbm.1) | copy-start | bytes 49156

commit v7 on v5

--- a/solution.py
+++ b/solution.py
@@ -12,7 +12,7 @@
 BF16 = jnp.bfloat16
 FWD = 16
 BWD = 6
-PIECES = 4
+PIECES = 6
 
 
 def dot(a, b):
@@ -46,8 +46,6 @@
     my_slab = lax.axis_index("slab")
     my_angle = lax.axis_index("angle")
 
-    far_first = sorted(range(1, n_angle), key=lambda d: -min(d, n_angle - d))
-
     def angle_peer(d):
         return lax.rem(my_angle + d, n_angle)
 
@@ -56,6 +54,11 @@
 
     vol_copy = pltpu.make_async_copy(vol_hbm, vol, local_sem.at[0])
     vol_copy.start()
+    barrier = pltpu.get_barrier_semaphore()
+    for d in range(1, n_angle):
+        pl.semaphore_signal(barrier, inc=1, device_id={"angle": angle_peer(d)}, device_id_type=MESH)
+    for d in range(1, n_slab):
+        pl.semaphore_signal(barrier, inc=1, device_id={"slab": slab_peer(d)}, device_id_type=MESH)
     index_copies = [
         pltpu.make_async_copy(voxel_hbm, voxel_v, local_sem.at[1]),
         pltpu.make_async_copy(tile_hbm, tile_v, local_sem.at[2]),
@@ -73,17 +76,12 @@
     meas_copy = pltpu.make_async_copy(meas_hbm, meas, local_sem.at[5])
     meas_copy.start()
 
-    barrier = pltpu.get_barrier_semaphore()
-    for d in range(1, n_angle):
-        pl.semaphore_signal(barrier, inc=1, device_id={"angle": angle_peer(d)}, device_id_type=MESH)
-    for d in range(1, n_slab):
-        pl.semaphore_signal(barrier, inc=1, device_id={"slab": slab_peer(d)}, device_id_type=MESH)
     vol_copy.wait()
     slab_vals[my_angle] = vol[...].astype(BF16)
     pl.semaphore_wait(barrier, n_angle + n_slab - 2)
 
     vals_copies = []
-    for d in far_first:
+    for d in range(1, n_angle):
         c = pltpu.make_async_remote_copy(
             src_ref=slab_vals.at[my_angle], dst_ref=slab_vals.at[my_angle],
             send_sem=vals_send.at[d - 1], recv_sem=vals_recv.at[d - 1],
@@ -106,7 +104,7 @@
 
     def angle_exchange(out, into, send, recv):
         copies = []
-        for d in far_first:
+        for d in range(1, n_angle):
             c = pltpu.make_async_remote_copy(
                 src_ref=out.at[angle_peer(d)], dst_ref=into.at[my_angle],
                 send_sem=send.at[d - 1], recv_sem=recv.at[d - 1],

time: 27 us -> 25.6 us (0.948)
  Pallas kernels: 23.4 us -> 22 us
    pallas_call x1, Pallas kernels: 23.4 us -> 22 us  [on_device(): pl.pallas_call(functools.partial(kernel, n_slab, n_angle, cap), out_shape...]
where the time goes in v7:
time: 25.6 us; the launch traced here: 25.4 us
  Pallas kernels  22 us (86%)
  local copies, waits for them, and re-layouts  1.38 us (5%)
  other arithmetic  1.33 us (5%)
  between operations  0.66 us (3%)
    pallas_call x1, Pallas kernels, on_device(): pl.pallas_call(functools.partial(kernel, n_slab, n_angle, cap), out_shape...  22 us
    unnamed x3, local copies, waits for them, and re-layouts  1.38 us
    add x1, other arithmetic, on_device(): return (volume + new, res)  1.33 us

profile of v7, /device:TPU:0, one launch (start us, length us, event | category | flops | bytes accessed | tf_op | source)
XLA Modules:
  0.0 25.4 jit_solution(18308079302827604210)
XLA Ops:
  0.6 0.0 copy-start
  0.6 22.0 %shard_map.77 = (f32[32,128]{1,0:T(8,128)}, f32[64,128]{1,0:T(8,128)}) custom-call(f32[32,128]{1,0:T(8,128)} %vol_hbm.1, f32[64,128]{1,0:T(8,128)} %meas_hbm.1, bf16[192,128,128]{2,1,0:T(8,128)(2,1)} %foot_hbm.1, s32[1,192]{1,0:T(1,128)} %bitcast.3, s32[1,192]{1,0:T(1,128)} %bitcast.4, s32[1,192]{1,0:T(1,128)} %bitcast.5), custom_call_target="tpu_custom_call" | custom-call | flops 25165824 | bytes 6291456 | tf_op jit(solution)/shard_map/pallas_call | solution.py:269
  22.7 0.0 copy-done
  22.7 1.3 %add.3 = f32[32,128]{1,0:T(8,128)} add(f32[32,128]{1,0:T(8,128)S(1)} %copy-done, f32[32,128]{1,0:T(8,128)} %get-tuple-element.4) | non-fusion elementwise | flops 4096 | bytes 49152 | tf_op jit(solution)/shard_map/add | solution.py:310
  24.0 1.4 %copy.9 = f32[64,128]{1,0:T(8,128)} copy(f32[64,128]{1,0:T(8,128)} %get-tuple-element.9) | data formatting | bytes 65536
Async XLA Ops:
  0.6 22.0 %copy-start = (f32[32,128]{1,0:T(8,128)S(1)}, f32[32,128]{1,0:T(8,128)}, u32[]{:S(2)}) copy-start(f32[32,128]{1,0:T(8,128)} %vol_hbm.1) | copy-start | bytes 49156

commit v8 on v4

--- a/solution.py
+++ b/solution.py
@@ -46,8 +46,6 @@
     my_slab = lax.axis_index("slab")
     my_angle = lax.axis_index("angle")
 
-    far_first = sorted(range(1, n_angle), key=lambda d: -min(d, n_angle - d))
-
     def angle_peer(d):
         return lax.rem(my_angle + d, n_angle)
 
@@ -56,6 +54,11 @@
 
     vol_copy = pltpu.make_async_copy(vol_hbm, vol, local_sem.at[0])
     vol_copy.start()
+    barrier = pltpu.get_barrier_semaphore()
+    for d in range(1, n_angle):
+        pl.semaphore_signal(barrier, inc=1, device_id={"angle": angle_peer(d)}, device_id_type=MESH)
+    for d in range(1, n_slab):
+        pl.semaphore_signal(barrier, inc=1, device_id={"slab": slab_peer(d)}, device_id_type=MESH)
     index_copies = [
         pltpu.make_async_copy(voxel_hbm, voxel_v, local_sem.at[1]),
         pltpu.make_async_copy(tile_hbm, tile_v, local_sem.at[2]),
@@ -73,17 +76,12 @@
     meas_copy = pltpu.make_async_copy(meas_hbm, meas, local_sem.at[5])
     meas_copy.start()
 
-    barrier = pltpu.get_barrier_semaphore()
-    for d in range(1, n_angle):
-        pl.semaphore_signal(barrier, inc=1, device_id={"angle": angle_peer(d)}, device_id_type=MESH)
-    for d in range(1, n_slab):
-        pl.semaphore_signal(barrier, inc=1, device_id={"slab": slab_peer(d)}, device_id_type=MESH)
     vol_copy.wait()
     slab_vals[my_angle] = vol[...].astype(BF16)
     pl.semaphore_wait(barrier, n_angle + n_slab - 2)
 
     vals_copies = []
-    for d in far_first:
+    for d in range(1, n_angle):
         c = pltpu.make_async_remote_copy(
             src_ref=slab_vals.at[my_angle], dst_ref=slab_vals.at[my_angle],
             send_sem=vals_send.at[d - 1], recv_sem=vals_recv.at[d - 1],
@@ -106,7 +104,7 @@
 
     def angle_exchange(out, into, send, recv):
         copies = []
-        for d in far_first:
+        for d in range(1, n_angle):
             c = pltpu.make_async_remote_copy(
                 src_ref=out.at[angle_peer(d)], dst_ref=into.at[my_angle],
                 send_sem=send.at[d - 1], recv_sem=recv.at[d - 1],
@@ -232,7 +230,7 @@
         return total * named
 
     back_copies = []
-    for d in far_first:
+    for d in range(1, n_angle):
         back_out[d] = residual_sums(angle_peer(d))
         c = pltpu.make_async_remote_copy(
             src_ref=back_out.at[d], dst_ref=back_in.at[my_angle],

time: 26.5 us -> 25.1 us (0.947)
  Pallas kernels: 22.9 us -> 21.5 us
    pallas_call x1, Pallas kernels: 22.9 us -> 21.5 us  [on_device(): pl.pallas_call(functools.partial(kernel, n_slab, n_angle, cap), out_shape...]
where the time goes in v8:
time: 25.1 us; the launch traced here: 24.9 us
  Pallas kernels  21.5 us (86%)
  local copies, waits for them, and re-layouts  1.38 us (5%)
  other arithmetic  1.33 us (5%)
  between operations  0.66 us (3%)
    pallas_call x1, Pallas kernels, on_device(): pl.pallas_call(functools.partial(kernel, n_slab, n_angle, cap), out_shape...  21.5 us
    unnamed x3, local copies, waits for them, and re-layouts  1.38 us
    add x1, other arithmetic, on_device(): return (volume + new, res)  1.33 us

profile of v8, /device:TPU:0, one launch (start us, length us, event | category | flops | bytes accessed | tf_op | source)
XLA Modules:
  0.0 24.9 jit_solution(5576855504485363464)
XLA Ops:
  0.6 0.0 copy-start
  0.6 21.5 %shard_map.77 = (f32[32,128]{1,0:T(8,128)}, f32[64,128]{1,0:T(8,128)}) custom-call(f32[32,128]{1,0:T(8,128)} %vol_hbm.1, f32[64,128]{1,0:T(8,128)} %meas_hbm.1, bf16[192,128,128]{2,1,0:T(8,128)(2,1)} %foot_hbm.1, s32[1,192]{1,0:T(1,128)} %bitcast.3, s32[1,192]{1,0:T(1,128)} %bitcast.4, s32[1,192]{1,0:T(1,128)} %bitcast.5), custom_call_target="tpu_custom_call" | custom-call | flops 25165824 | bytes 6291456 | tf_op jit(solution)/shard_map/pallas_call | solution.py:280
  22.2 0.0 copy-done
  22.2 1.3 %add.3 = f32[32,128]{1,0:T(8,128)} add(f32[32,128]{1,0:T(8,128)S(1)} %copy-done, f32[32,128]{1,0:T(8,128)} %get-tuple-element.4) | non-fusion elementwise | flops 4096 | bytes 49152 | tf_op jit(solution)/shard_map/add | solution.py:321
  23.5 1.4 %copy.9 = f32[64,128]{1,0:T(8,128)} copy(f32[64,128]{1,0:T(8,128)} %get-tuple-element.9) | data formatting | bytes 65536
Async XLA Ops:
  0.6 21.5 %copy-start = (f32[32,128]{1,0:T(8,128)S(1)}, f32[32,128]{1,0:T(8,128)}, u32[]{:S(2)}) copy-start(f32[32,128]{1,0:T(8,128)} %vol_hbm.1) | copy-start | bytes 49156
